TPU v7x, 256 devices: a whole 4x4x8 slice. The times are simulated.
256 devices in a mesh: gx: 8 (over x, core), gy: 4 (over y), band: 8 (over z).
Axes of the slice: x: 4, y: 4, z: 8, core: 2. Of those that a mesh axis runs over, the one named last changes fastest.
Arguments:
- orbitals: float32 [160, 48, 32, 128], P('band', 'gx', 'gy'), may hold values from -6 to 6
- potential: float32 [48, 32, 128], P('gx', 'gy'), may hold values from -1 to 1
Outputs:
- filtered: float32 [160, 48, 32, 128], P('band', 'gx', 'gy')
- correlation: float32 [160, 160], P('band')
- projected: float32 [160, 160], P('band')
All inputs are finite; a program needn't handle non-finite values.
Results may differ from a plain program's by a relative error of at most 0.000051.
Values sent between devices are 32-bit elements; how exact they have to be, the bound alone decides.
A program may use at most 64 MiB of HBM per device.

v0:
```python
import functools

import jax
import jax.numpy as jnp
from jax import lax
from jax.experimental import pallas as pl
from jax.experimental.pallas import tpu as pltpu
from jax.sharding import PartitionSpec as P

stencil_weights = (
    -5369.0 / 1800.0,
    12.0 / 7.0,
    -15.0 / 56.0,
    10.0 / 189.0,
    -1.0 / 112.0,
    2.0 / 1925.0,
    -1.0 / 16632.0,
)
center_level = 7.5
half_width = 4.5

MESH = pl.DeviceIdType.MESH
F32 = jnp.float32
PART = 4


def kernel(
    dims,
    scale,
    v_ref,
    pot_ref,
    filt_ref,
    corr_ref,
    proj_ref,
    own,
    tall,
    xlo,
    xhi,
    diag,
    stage,
    gather,
    rows_out,
    rows_in,
    gx_in,
    gy_in,
    load_sem,
    halo_send,
    halo_recv,
    z_send,
    z_recv,
    r_send,
    r_recv,
    s_send,
    s_recv,
):
    ngx, ngy, nb = dims
    norb, wx, wy, nz = v_ref.shape
    chunks = norb // PART
    gx, gy, band = lax.axis_index("gx"), lax.axis_index("gy"), lax.axis_index("band")

    load = pltpu.make_async_copy(v_ref, own.at[0], load_sem)
    load.start()

    barrier = pltpu.get_barrier_semaphore()
    for d in range(1, ngx):
        pl.semaphore_signal(barrier, 1, device_id={"gx": lax.rem(gx + d, ngx)}, device_id_type=MESH)
    for d in range(1, ngy):
        pl.semaphore_signal(barrier, 1, device_id={"gy": lax.rem(gy + d, ngy)}, device_id_type=MESH)
    for d in range(1, nb):
        pl.semaphore_signal(barrier, 1, device_id={"band": lax.rem(band + d, nb)}, device_id_type=MESH)

    diag[...] = (pot_ref[...] - 1.5 * stencil_weights[0] - center_level) * (1.0 / half_width)
    taps = [0.0] + [-0.5 * w / half_width for w in stencil_weights[1:]]
    lane = lax.broadcasted_iota(jnp.int32, (wy, nz), 1)

    load.wait()

    def fill(n, carry):
        for x in range(wx):
            tall[0, n, x, 8:16] = own[0, n, x]
        return carry

    lax.fori_loop(0, norb, fill, 0)
    pl.semaphore_wait(barrier, ngx + ngy + nb - 3)

    sides = (
        {"gx": lax.rem(gx + 1, ngx)},
        {"gx": lax.rem(gx + ngx - 1, ngx)},
        {"gy": lax.rem(gy + 1, ngy)},
        {"gy": lax.rem(gy + ngy - 1, ngy)},
    )

    def halo_copy(level, start, count, sem_at, side):
        group = pl.ds(start, count)
        if side == 0:
            src, dst = own.at[level, group], xlo.at[level, group]
        elif side == 1:
            src, dst = own.at[level, group], xhi.at[level, group]
        elif side == 2:
            src, dst = own.at[level, group, :, 2:8], tall.at[level, group, :, 2:8]
        else:
            src, dst = own.at[level, group, :, 0:6], tall.at[level, group, :, 16:22]
        return pltpu.make_async_remote_copy(
            src_ref=src,
            dst_ref=dst,
            send_sem=halo_send.at[level, side],
            recv_sem=halo_recv.at[level, sem_at, side],
            device_id=sides[side],
            device_id_type=MESH,
        )

    def halo_start(level, c):
        for side in (2, 3, 0, 1):
            halo_copy(level, c * PART, PART, c, side).start()

    def halo_wait(level, c):
        for side in (0, 1, 2, 3):
            halo_copy(level, c * PART, PART, c, side).wait_recv()

    def base(level, n):
        line = (
            [xlo[level, n, x] for x in range(wx)]
            + [own[level, n, x] for x in range(wx)]
            + [xhi[level, n, x] for x in range(wx)]
        )
        out = []
        for x in range(wx):
            v = line[wx + x]
            total = diag[x] * v
            for k in range(1, 7):
                near = line[wx + x + k] + line[wx + x - k]
                near += tall[level, n, x, 8 + k : 16 + k] + tall[level, n, x, 8 - k : 16 - k]
                near += jnp.where(lane < nz - k, pltpu.roll(v, nz - k, 1), 0.0)
                near += jnp.where(lane >= k, pltpu.roll(v, k, 1), 0.0)
                total += taps[k] * near
            out.append(total)
        return out

    def z_start(which, c):
        for d in range(1, nb):
            peer = lax.rem(band + d, nb)
            pltpu.make_async_remote_copy(
                src_ref=stage.at[which, c, peer],
                dst_ref=gather.at[which, pl.ds(pl.multiple_of(band * (norb * wx) + c * (PART * wx), 8), PART * wx)],
                send_sem=z_send.at[which],
                recv_sem=z_recv.at[which],
                device_id={"band": peer},
                device_id_type=MESH,
            ).start()

    def spread(which, c, value):
        turned = jnp.swapaxes(value, 0, 1)
        stage[which, c] = turned
        mine = pl.ds(pl.multiple_of(band * (norb * wx) + c * (PART * wx), 8), PART * wx)
        gather[which, mine] = stage[which, c, band]

    def first_sends(c, carry):
        halo_start(0, c)
        return carry

    lax.fori_loop(0, chunks, first_sends, 0)

    def step(level, c):
        halo_wait(level, c)

        def one(i, carry):
            n = c * PART + i
            for x, value in enumerate(base(level, n)):
                if level > 0:
                    value = 2.0 * value - own[level - 1, n, x]
                own[level + 1, n, x] = value
                tall[level + 1, n, x, 8:16] = value
            return carry

        lax.fori_loop(0, PART, one, 0)
        halo_start(level + 1, c)
        if level == 2:
            block = own[3, pl.ds(c * PART, PART)].reshape(PART * wx, wy, nz)
            spread(0, c, block)
            z_start(0, c)

    for level in range(3):
        def body(c, carry, level=level):
            step(level, c)
            return carry

        lax.fori_loop(0, chunks, body, 0)

    save = pltpu.make_async_copy(own.at[3], filt_ref, load_sem)
    save.start()

    def last(c, carry):
        halo_wait(3, c)

        def one(i, carry):
            n = c * PART + i
            for x, value in enumerate(base(3, n)):
                own[4, n, x] = half_width * value + center_level * own[3, n, x]
            return carry

        lax.fori_loop(0, PART, one, 0)
        block = own[4, pl.ds(c * PART, PART)].reshape(PART * wx, wy, nz)
        spread(1, c, block)
        z_start(1, c)
        return carry

    lax.fori_loop(0, chunks, last, 0)

    share = norb * wx * (nb - 1)

    def z_done(which):
        return pltpu.make_async_remote_copy(
            src_ref=gather.at[which, pl.ds(0, share)],
            dst_ref=gather.at[which, pl.ds(0, share)],
            send_sem=z_send.at[which],
            recv_sem=z_recv.at[which],
            device_id={"band": lax.rem(band + 1, nb)},
            device_id_type=MESH,
        )

    total_orbs = norb * nb

    def operand(which):
        return jnp.concatenate(
            [gather[which, pl.ds(x, total_orbs, stride=wx), :] for x in range(wx)], axis=1
        )

    def product(a, b):
        return lax.dot_general(
            a, b, (((1,), (1,)), ((), ())), precision=lax.Precision.HIGHEST, preferred_element_type=F32
        )

    def rows_copy(which, peer):
        return pltpu.make_async_remote_copy(
            src_ref=rows_out.at[which, peer],
            dst_ref=rows_in.at[which, band],
            send_sem=r_send.at[which],
            recv_sem=r_recv.at[which],
            device_id={"band": peer},
            device_id_type=MESH,
        )

    def rows_done(which):
        return pltpu.make_async_remote_copy(
            src_ref=rows_in.at[which, pl.ds(0, nb - 1)],
            dst_ref=rows_in.at[which, pl.ds(0, nb - 1)],
            send_sem=r_send.at[which],
            recv_sem=r_recv.at[which],
            device_id={"band": lax.rem(band + 1, nb)},
            device_id_type=MESH,
        )

    def scatter(which, value):
        rows_out[which] = value.reshape(nb, norb, total_orbs)
        rows_in[which, band] = rows_out[which, band]
        for d in range(1, nb):
            rows_copy(which, lax.rem(band + d, nb)).start()

    z_done(0).wait_recv()
    scatter(0, product(operand(0), operand(0)))
    z_done(1).wait_recv()
    scatter(1, product(operand(1), operand(0)))

    def ordered(ref, count):
        value = ref[0]
        for i in range(1, count):
            value = value + ref[i]
        return value

    for which in range(2):
        rows_done(which).wait_recv()
        value = rows_in[which, 0]
        for i in range(1, nb):
            value = value + rows_in[which, i]
        gx_in[gx, which] = value

    def gx_copy(peer):
        return pltpu.make_async_remote_copy(
            src_ref=gx_in.at[gx],
            dst_ref=gx_in.at[gx],
            send_sem=s_send.at[0],
            recv_sem=s_recv.at[0],
            device_id={"gx": peer},
            device_id_type=MESH,
        )

    for d in range(1, ngx):
        gx_copy(lax.rem(gx + d, ngx)).start()
    gx_done = pltpu.make_async_remote_copy(
        src_ref=gx_in.at[pl.ds(0, ngx - 1)],
        dst_ref=gx_in.at[pl.ds(0, ngx - 1)],
        send_sem=s_send.at[0],
        recv_sem=s_recv.at[0],
        device_id={"gx": lax.rem(gx + 1, ngx)},
        device_id_type=MESH,
    )
    gx_done.wait_recv()
    gy_in[gy] = ordered(gx_in, ngx)

    for d in range(1, ngy):
        pltpu.make_async_remote_copy(
            src_ref=gy_in.at[gy],
            dst_ref=gy_in.at[gy],
            send_sem=s_send.at[1],
            recv_sem=s_recv.at[1],
            device_id={"gy": lax.rem(gy + d, ngy)},
            device_id_type=MESH,
        ).start()
    gy_done = pltpu.make_async_remote_copy(
        src_ref=gy_in.at[pl.ds(0, ngy - 1)],
        dst_ref=gy_in.at[pl.ds(0, ngy - 1)],
        send_sem=s_send.at[1],
        recv_sem=s_recv.at[1],
        device_id={"gy": lax.rem(gy + 1, ngy)},
        device_id_type=MESH,
    )
    gy_done.wait_recv()
    sums = ordered(gy_in, ngy) * scale
    corr_ref[...] = sums[0]
    proj_ref[...] = sums[1]

    for level in range(4):
        for side in range(4):
            halo_copy(level, 0, norb, 0, side).wait_send()
    for which in range(2):
        z_done(which).wait_send()
        rows_done(which).wait_send()
    gx_done.wait_send()
    gy_done.wait_send()
    save.wait()


def body(orbitals, potential):
    norb, wx, wy, nz = orbitals.shape
    ngx, ngy, nb = lax.axis_size("gx"), lax.axis_size("gy"), lax.axis_size("band")
    total = norb * nb
    chunks = norb // PART
    scale = 1.0 / (wx * wy * nz * ngx * ngy)
    block = (norb, wx, wy, nz)
    vmem = pl.BlockSpec(memory_space=pltpu.VMEM)
    hbm = pl.BlockSpec(memory_space=pl.ANY)
    return pl.pallas_call(
        functools.partial(kernel, (ngx, ngy, nb), scale),
        out_shape=(
            jax.ShapeDtypeStruct(block, F32),
            jax.ShapeDtypeStruct((norb, total), F32),
            jax.ShapeDtypeStruct((norb, total), F32),
        ),
        in_specs=[hbm, vmem],
        out_specs=(hbm, vmem, vmem),
        scratch_shapes=[
            pltpu.VMEM((5,) + block, F32),
            pltpu.VMEM((4, norb, wx, 24, nz), F32),
            pltpu.VMEM((4,) + block, F32),
            pltpu.VMEM((4,) + block, F32),
            pltpu.VMEM((wx, wy, nz), F32),
            pltpu.VMEM((2, chunks, nb, PART * wx, nz), F32),
            pltpu.VMEM((2, total * wx, nz), F32),
            pltpu.VMEM((2, nb, norb, total), F32),
            pltpu.VMEM((2, nb, norb, total), F32),
            pltpu.VMEM((ngx, 2, norb, total), F32),
            pltpu.VMEM((ngy, 2, norb, total), F32),
            pltpu.SemaphoreType.DMA,
            pltpu.SemaphoreType.DMA((4, 4)),
            pltpu.SemaphoreType.DMA((4, chunks, 4)),
            pltpu.SemaphoreType.DMA((2,)),
            pltpu.SemaphoreType.DMA((2,)),
            pltpu.SemaphoreType.DMA((2,)),
            pltpu.SemaphoreType.DMA((2,)),
            pltpu.SemaphoreType.DMA((2,)),
            pltpu.SemaphoreType.DMA((2,)),
        ],
        compiler_params=pltpu.CompilerParams(
            collective_id=0, has_side_effects=True, vmem_limit_bytes=48 * 1024 * 1024
        ),
        cost_estimate=pl.CostEstimate(flops=200_000_000, bytes_accessed=2_000_000, transcendentals=0),
    )(orbitals, potential)


def solution(mesh):
    in_specs = (P("band", "gx", "gy", None), P("gx", "gy", None))
    out_specs = (P("band", "gx", "gy", None), P("band", None), P("band", None))
    return jax.shard_map(body, mesh=mesh, in_specs=in_specs, out_specs=out_specs, check_vma=False)
```

profile of v0, /device:TPU:1, one launch (start us, length us, event | category | flops | bytes accessed | tf_op | source)
XLA Modules:
  0.0 80.2 jit_solution(224303085849340591)
XLA Ops:
  0.6 0.0 copy-start
  0.6 1.0 %copy-done = f32[20,6,8,128]{3,2,1,0:T(8,128)S(1)} copy-done((f32[20,6,8,128]{3,2,1,0:T(8,128)S(1)}, f32[20,6,8,128]{3,2,1,0:T(8,128)}, u32[]{:S(2)}) %copy-start) | copy-done | bytes 491544
  1.7 0.0 copy-start.1
  1.7 0.7 copy-done.1
  2.4 75.8 %shard_map.49 = (f32[20,6,8,128]{3,2,1,0:T(8,128)S(1)}, f32[20,160]{1,0:T(8,128)S(1)}, f32[20,160]{1,0:T(8,128)S(1)}) custom-call(f32[20,6,8,128]{3,2,1,0:T(8,128)S(1)} %copy-done, f32[6,8,128]{2,1,0:T(8,128)S(1)} %copy-done.1), custom_call_target="tpu_custom_call" | custom-call | flops 200000000 | bytes 2000000 | tf_op jit(solution)/shard_map/pallas_call | solution.py:342
  78.2 0.8 copy.8
  79.0 0.6 copy.9
  79.6 0.6 copy.10
Async XLA Ops:
  0.6 1.0 %copy-start = (f32[20,6,8,128]{3,2,1,0:T(8,128)S(1)}, f32[20,6,8,128]{3,2,1,0:T(8,128)}, u32[]{:S(2)}) copy-start(f32[20,6,8,128]{3,2,1,0:T(8,128)} %v_ref.1) | copy-start | bytes 1474564
  1.7 0.7 copy-start.1
where the time goes:
time: 80.4 us; the launch traced here: 80.2 us
  Pallas kernels  75.8 us (94%)
  local copies, waits for them, and re-layouts  3.76 us (5%)
    pallas_call x1, Pallas kernels, body(): pl.pallas_call(functools.partial(kernel, (ngx, ngy, nb), scale), out_shap...  75.8 us
    unnamed x7, local copies, waits for them, and re-layouts  3.76 us

commit v1 on v0

v1 whole, which is shorter than its diff:
```python
import functools

import jax
import jax.numpy as jnp
from jax import lax
from jax.experimental import pallas as pl
from jax.experimental.pallas import tpu as pltpu
from jax.sharding import PartitionSpec as P

stencil_weights = (
    -5369.0 / 1800.0,
    12.0 / 7.0,
    -15.0 / 56.0,
    10.0 / 189.0,
    -1.0 / 112.0,
    2.0 / 1925.0,
    -1.0 / 16632.0,
)
center_level = 7.5
half_width = 4.5

MESH = pl.DeviceIdType.MESH
F32 = jnp.float32
PART = 4


def kernel(
    dims,
    scale,
    v_ref,
    pot_ref,
    filt_ref,
    corr_ref,
    proj_ref,
    own,
    tall,
    xlo,
    xhi,
    diag,
    shift_w,
    stage,
    gather,
    tail,
    rows_out,
    rows_in,
    gx_in,
    gy_in,
    load_sem,
    ready,
    halo_send,
    halo_recv,
    z_send,
    z_recv,
    r_send,
    r_recv,
    s_send,
    s_recv,
):
    ngx, ngy, nb = dims
    norb, wx, wy, nz = own.shape[1:]
    chunks = norb // PART
    total_orbs = norb * nb
    half_x, half_y = wx // 2, wy // 2
    gx, gy, band = lax.axis_index("gx"), lax.axis_index("gy"), lax.axis_index("band")

    load = pltpu.make_async_copy(v_ref, own.at[0], load_sem.at[0])
    load.start()
    load_pot = pltpu.make_async_copy(pot_ref, diag, load_sem.at[1])
    load_pot.start()

    sides = (
        {"gx": lax.rem(gx + 1, ngx)},
        {"gx": lax.rem(gx + ngx - 1, ngx)},
        {"gy": lax.rem(gy + 1, ngy)},
        {"gy": lax.rem(gy + ngy - 1, ngy)},
        {"band": lax.rem(band + 1, nb)},
        {"band": lax.rem(band + nb - 1, nb)},
    )

    def clear(n, carry):
        for x in range(wx):
            xlo[3, n, x, 0:half_y] = jnp.zeros((half_y, nz), F32)
            xhi[3, n, x, half_y:wy] = jnp.zeros((wy - half_y, nz), F32)
            if x < half_x:
                tall[3, n, x, 0:8] = jnp.zeros((8, nz), F32)
            else:
                tall[3, n, x, 16:24] = jnp.zeros((8, nz), F32)
        return carry

    lax.fori_loop(0, norb, clear, 0)

    barrier = pltpu.get_barrier_semaphore()
    for peer in sides:
        pl.semaphore_signal(barrier, 1, device_id=peer, device_id_type=MESH)

    taps = [0.0] + [-0.5 * w / half_width for w in stencil_weights[1:]]
    lane = lax.broadcasted_iota(jnp.int32, (wy, nz), 1)

    spots = (
        [(0, j) for j in (-2, -1, 1, 2)]
        + [(5, j) for j in (-2, -1, 0, 1)]
        + [(-5, j) for j in (-1, 0, 1, 2)]
    )
    for i, (far, j) in enumerate(spots):
        where = lane + far
        where = jnp.where(where >= nz, where - nz, jnp.where(where < 0, where + nz, where))
        source = where - (far + j)
        inside = jnp.logical_and(source >= 0, source < nz)
        shift_w[i] = jnp.where(inside, taps[abs(far + j)], 0.0)

    tail[...] = jnp.zeros_like(tail)
    load.wait()
    load_pot.wait()
    diag[...] = (diag[...] - 1.5 * stencil_weights[0] - center_level) * (1.0 / half_width)

    def fill(n, carry):
        for x in range(wx):
            tall[0, n, x, 8:16] = own[0, n, x]
        return carry

    lax.fori_loop(0, norb, fill, 0)
    pl.semaphore_wait(barrier, 6)

    def relay(turn):
        for peer in sides:
            pl.semaphore_signal(ready.at[turn], 1, device_id=peer, device_id_type=MESH)

    def heard(turn):
        pl.semaphore_wait(ready.at[turn], 6)

    def halo_copy(level, start, count, sem_at, side):
        group = pl.ds(start, count)
        if level < 3:
            src = (
                own.at[level, group],
                own.at[level, group],
                own.at[level, group, :, 2:8],
                own.at[level, group, :, 0:6],
            )[side]
            dst = (
                xlo.at[level, group],
                xhi.at[level, group],
                tall.at[level, group, :, 2:8],
                tall.at[level, group, :, 16:22],
            )[side]
        else:
            src = (
                own.at[level, group, :, half_y:wy],
                own.at[level, group, :, 0:half_y],
                own.at[level, group, half_x:wx, 2:8],
                own.at[level, group, 0:half_x, 0:6],
            )[side]
            dst = (
                xlo.at[level, group, :, half_y:wy],
                xhi.at[level, group, :, 0:half_y],
                tall.at[level, group, half_x:wx, 2:8],
                tall.at[level, group, 0:half_x, 16:22],
            )[side]
        return pltpu.make_async_remote_copy(
            src_ref=src,
            dst_ref=dst,
            send_sem=halo_send.at[level, side],
            recv_sem=halo_recv.at[level, sem_at, side],
            device_id=sides[side],
            device_id_type=MESH,
        )

    def halo_start(level, c):
        for side in (2, 3, 0, 1):
            halo_copy(level, c * PART, PART, c, side).start()

    def halo_wait(level, c):
        for side in (0, 1, 2, 3):
            halo_copy(level, c * PART, PART, c, side).wait_recv()

    def base(level, n):
        inner = [own[level, n, x] for x in range(wx)]
        if level == 3:
            inner = [0.5 * v for v in inner]
        line = [xlo[level, n, x] for x in range(wx)] + inner + [xhi[level, n, x] for x in range(wx)]
        out = []
        for x in range(wx):
            v = inner[x]
            total = diag[x] * v
            for k in range(1, 7):
                near = line[wx + x + k] + line[wx + x - k]
                near += tall[level, n, x, 8 + k : 16 + k] + tall[level, n, x, 8 - k : 16 - k]
                total += taps[k] * near
            rolled = {0: v}
            for j in (-2, -1, 1, 2):
                rolled[j] = pltpu.roll(v, j % nz, 1)
            parts = {0: None, 5: None, -5: None}
            for i, (far, j) in enumerate(spots):
                term = shift_w[i] * rolled[j]
                parts[far] = term if parts[far] is None else parts[far] + term
            total += parts[0]
            total += pltpu.roll(parts[5], 5, 1) + pltpu.roll(parts[-5], nz - 5, 1)
            out.append(total)
        return out

    def z_rows(c):
        return pl.ds(pl.multiple_of(band * (norb * wx) + c * (PART * wx), 8), PART * wx)

    def spread(which, c, value):
        stage[which, c] = jnp.swapaxes(value, 0, 1)
        gather[which, z_rows(c)] = stage[which, c, band]
        for d in (1, 2, 3, 4, -1, -2, -3):
            peer = lax.rem(band + d + nb, nb)
            pltpu.make_async_remote_copy(
                src_ref=stage.at[which, c, peer],
                dst_ref=gather.at[which, z_rows(c)],
                send_sem=z_send.at[which],
                recv_sem=z_recv.at[which],
                device_id={"band": peer},
                device_id_type=MESH,
            ).start()

    def step(level, c):
        halo_wait(level, c)

        def one(i, carry):
            n = c * PART + i
            for x, value in enumerate(base(level, n)):
                if level in (1, 2):
                    value = 2.0 * value - own[level - 1, n, x]
                elif level == 3:
                    value = half_width * value + (0.5 * center_level) * own[3, n, x]
                own[level + 1, n, x] = value
                if level < 3:
                    tall[level + 1, n, x, 8:16] = 0.5 * value if level == 2 else value
            return carry

        lax.fori_loop(0, PART, one, 0)
        if level < 3:
            halo_start(level + 1, c)
        if level >= 2:
            spread(level - 2, c, own[level + 1, pl.ds(c * PART, PART)].reshape(PART * wx, wy, nz))

    def run(level, first, end):
        def body(c, carry):
            if level < 0:
                halo_start(0, c)
            else:
                step(level, c)
            return carry

        lax.fori_loop(first, end, body, 0)

    cut = (chunks + 1) // 2
    run(-1, 0, cut)
    relay(0)
    heard(0)
    relay(1)
    run(0, 0, cut)
    heard(1)
    relay(2)
    run(1, 0, cut)
    run(-1, cut, chunks)
    heard(2)
    run(2, 0, cut)
    run(0, cut, chunks)
    run(3, 0, cut)
    run(1, cut, chunks)
    run(2, cut, chunks)
    save = pltpu.make_async_copy(own.at[3], filt_ref, load_sem.at[0])
    save.start()
    run(3, cut, chunks)

    def all_of(ref, count, send, recv, peer):
        part = ref.at[pl.ds(0, count)]
        return pltpu.make_async_remote_copy(
            src_ref=part, dst_ref=part, send_sem=send, recv_sem=recv, device_id=peer, device_id_type=MESH
        )

    def z_done(which):
        return all_of(gather.at[which], norb * wx * (nb - 1), z_send.at[which], z_recv.at[which], sides[4])

    def rows_done(which):
        return all_of(rows_in.at[which], nb - 1, r_send.at[which], r_recv.at[which], sides[4])

    def gx_done(which):
        return all_of(gx_in.at[which], ngx - 1, s_send.at[which, 0], s_recv.at[which, 0], sides[0])

    def gy_done(which):
        return all_of(gy_in.at[which], ngy - 1, s_send.at[which, 1], s_recv.at[which, 1], sides[2])

    def operand(which):
        return jnp.concatenate(
            [gather[which, pl.ds(x, total_orbs, stride=wx), :] for x in range(wx)], axis=1
        )

    def product(a, b):
        return lax.dot_general(
            a, b, (((1,), (1,)), ((), ())), precision=lax.Precision.HIGHEST, preferred_element_type=F32
        )

    def scatter(which, value):
        blocks = value.reshape(nb, norb, total_orbs)
        rows_out[which, :, 0:norb] = blocks[:, :, 0:128]
        tail[:, 0:norb, 0:32] = blocks[:, :, 128:160]
        for b in range(nb):
            packed = tail[b, 0:8] + pltpu.roll(tail[b, 8:16], 32, 1) + pltpu.roll(tail[b, 16:24], 64, 1)
            rows_out[which, b, 24:32] = packed
        rows_in[which, band] = rows_out[which, band]
        for d in (1, 2, 3, 4, -1, -2, -3):
            peer = lax.rem(band + d + nb, nb)
            pltpu.make_async_remote_copy(
                src_ref=rows_out.at[which, peer],
                dst_ref=rows_in.at[which, band],
                send_sem=r_send.at[which],
                recv_sem=r_recv.at[which],
                device_id={"band": peer},
                device_id_type=MESH,
            ).start()

    def ordered(ref, count):
        value = ref[0]
        for i in range(1, count):
            value = value + ref[i]
        return value

    def over_gx(which):
        rows_done(which).wait_recv()
        gx_in[which, gx] = ordered(rows_in.at[which], nb)
        for d in range(1, ngx):
            pltpu.make_async_remote_copy(
                src_ref=gx_in.at[which, gx],
                dst_ref=gx_in.at[which, gx],
                send_sem=s_send.at[which, 0],
                recv_sem=s_recv.at[which, 0],
                device_id={"gx": lax.rem(gx + d, ngx)},
                device_id_type=MESH,
            ).start()

    def over_gy(which):
        gx_done(which).wait_recv()
        gy_in[which, gy] = ordered(gx_in.at[which], ngx)
        for d in range(1, ngy):
            pltpu.make_async_remote_copy(
                src_ref=gy_in.at[which, gy],
                dst_ref=gy_in.at[which, gy],
                send_sem=s_send.at[which, 1],
                recv_sem=s_recv.at[which, 1],
                device_id={"gy": lax.rem(gy + d, ngy)},
                device_id_type=MESH,
            ).start()

    def finish(which, out):
        gy_done(which).wait_recv()
        value = ordered(gy_in.at[which], ngy) * scale
        out[:, 0:128] = value[0:norb]
        rest = value[24:32]
        out[0:8, 128:160] = rest[:, 0:32]
        out[8:16, 128:160] = pltpu.roll(rest, 96, 1)[:, 0:32]
        out[16:20, 128:160] = pltpu.roll(rest, 64, 1)[0:4, 0:32]

    z_done(0).wait_recv()
    scatter(0, product(operand(0), operand(0)))
    over_gx(0)
    z_done(1).wait_recv()
    one_way = product(operand(0), operand(1))
    scatter(1, one_way + one_way.T)
    over_gy(0)
    over_gx(1)
    finish(0, corr_ref)
    over_gy(1)
    finish(1, proj_ref)

    for level in range(4):
        for side in range(4):
            halo_copy(level, 0, norb, 0, side).wait_send()
    for which in range(2):
        z_done(which).wait_send()
        rows_done(which).wait_send()
        gx_done(which).wait_send()
        gy_done(which).wait_send()
    save.wait()


def body(orbitals, potential):
    norb, wx, wy, nz = orbitals.shape
    ngx, ngy, nb = lax.axis_size("gx"), lax.axis_size("gy"), lax.axis_size("band")
    total = norb * nb
    chunks = norb // PART
    scale = 1.0 / (wx * wy * nz * ngx * ngy)
    block = (norb, wx, wy, nz)
    vmem = pl.BlockSpec(memory_space=pltpu.VMEM)
    hbm = pl.BlockSpec(memory_space=pltpu.HBM)
    return pl.pallas_call(
        functools.partial(kernel, (ngx, ngy, nb), scale),
        out_shape=(
            jax.ShapeDtypeStruct(block, F32),
            jax.ShapeDtypeStruct((norb, total), F32),
            jax.ShapeDtypeStruct((norb, total), F32),
        ),
        in_specs=[hbm, hbm],
        out_specs=(hbm, vmem, vmem),
        scratch_shapes=[
            pltpu.VMEM((5,) + block, F32),
            pltpu.VMEM((4, norb, wx, 24, nz), F32),
            pltpu.VMEM((4,) + block, F32),
            pltpu.VMEM((4,) + block, F32),
            pltpu.VMEM((wx, wy, nz), F32),
            pltpu.VMEM((12, wy, nz), F32),
            pltpu.VMEM((2, chunks, nb, PART * wx, nz), F32),
            pltpu.VMEM((2, total * wx, nz), F32),
            pltpu.VMEM((nb, 24, 128), F32),
            pltpu.VMEM((2, nb, 32, 128), F32),
            pltpu.VMEM((2, nb, 32, 128), F32),
            pltpu.VMEM((2, ngx, 32, 128), F32),
            pltpu.VMEM((2, ngy, 32, 128), F32),
            pltpu.SemaphoreType.DMA((2,)),
            pltpu.SemaphoreType.REGULAR((3,)),
            pltpu.SemaphoreType.DMA((4, 4)),
            pltpu.SemaphoreType.DMA((4, chunks, 4)),
            pltpu.SemaphoreType.DMA((2,)),
            pltpu.SemaphoreType.DMA((2,)),
            pltpu.SemaphoreType.DMA((2,)),
            pltpu.SemaphoreType.DMA((2,)),
            pltpu.SemaphoreType.DMA((2, 2)),
            pltpu.SemaphoreType.DMA((2, 2)),
        ],
        compiler_params=pltpu.CompilerParams(
            collective_id=0, has_side_effects=True, vmem_limit_bytes=48 * 1024 * 1024
        ),
        cost_estimate=pl.CostEstimate(flops=200_000_000, bytes_accessed=2_000_000, transcendentals=0),
    )(orbitals, potential)


def solution(mesh):
    in_specs = (P("band", "gx", "gy", None), P("gx", "gy", None))
    out_specs = (P("band", "gx", "gy", None), P("band", None), P("band", None))
    return jax.shard_map(body, mesh=mesh, in_specs=in_specs, out_specs=out_specs, check_vma=False)
```

time: 80.4 us -> 75.6 us (0.940)
  Pallas kernels: 75.8 us -> 71 us
    pallas_call x1, Pallas kernels: 75.8 us -> 71 us  [body(): pl.pallas_call(functools.partial(kernel, (ngx, ngy, nb), scale), out_shap...]
where the time goes in v1:
time: 75.6 us; the launch traced here: 75.4 us
  Pallas kernels  71 us (94%)
  local copies, waits for them, and re-layouts  3.76 us (5%)
    pallas_call x1, Pallas kernels, body(): pl.pallas_call(functools.partial(kernel, (ngx, ngy, nb), scale), out_shap...  71 us
    unnamed x7, local copies, waits for them, and re-layouts  3.76 us

profile of v1, /device:TPU:1, one launch (start us, length us, event | category | flops | bytes accessed | tf_op | source)
XLA Modules:
  0.0 75.4 jit_solution(14320701379352482523)
XLA Ops:
  0.6 0.0 copy-start
  0.6 1.0 %copy-done = f32[20,6,8,128]{3,2,1,0:T(8,128)S(1)} copy-done((f32[20,6,8,128]{3,2,1,0:T(8,128)S(1)}, f32[20,6,8,128]{3,2,1,0:T(8,128)}, u32[]{:S(2)}) %copy-start) | copy-done | bytes 491544
  1.7 0.0 copy-start.1
  1.7 0.7 copy-done.1
  2.4 71.0 %shard_map.49 = (f32[20,6,8,128]{3,2,1,0:T(8,128)S(1)}, f32[20,160]{1,0:T(8,128)S(1)}, f32[20,160]{1,0:T(8,128)S(1)}) custom-call(f32[20,6,8,128]{3,2,1,0:T(8,128)S(1)} %copy-done, f32[6,8,128]{2,1,0:T(8,128)S(1)} %copy-done.1), custom_call_target="tpu_custom_call" | custom-call | flops 200000000 | bytes 2000000 | tf_op jit(solution)/shard_map/pallas_call | solution.py:389
  73.4 0.8 %copy.8 = f32[20,6,8,128]{3,2,1,0:T(8,128)} copy(f32[20,6,8,128]{3,2,1,0:T(8,128)S(1)} %get-tuple-element.6) | data formatting | bytes 983040
  74.2 0.6 copy.9
  74.8 0.6 copy.10
Async XLA Ops:
  0.6 1.0 %copy-start = (f32[20,6,8,128]{3,2,1,0:T(8,128)S(1)}, f32[20,6,8,128]{3,2,1,0:T(8,128)}, u32[]{:S(2)}) copy-start(f32[20,6,8,128]{3,2,1,0:T(8,128)} %v_ref.1) | copy-start | bytes 1474564
  1.7 0.7 copy-start.1

commit v2 on v1

--- a/solution.py
+++ b/solution.py
@@ -30,8 +30,7 @@
     v_ref,
     pot_ref,
     filt_ref,
-    corr_ref,
-    proj_ref,
+    sums_ref,
     own,
     tall,
     xlo,
@@ -230,7 +229,7 @@
                     tall[level + 1, n, x, 8:16] = 0.5 * value if level == 2 else value
             return carry
 
-        lax.fori_loop(0, PART, one, 0)
+        lax.fori_loop(0, PART, one, 0, unroll=4)
         if level < 3:
             halo_start(level + 1, c)
         if level >= 2:
@@ -345,26 +344,21 @@
                 device_id_type=MESH,
             ).start()
 
-    def finish(which, out):
+    def finish(which):
         gy_done(which).wait_recv()
-        value = ordered(gy_in.at[which], ngy) * scale
-        out[:, 0:128] = value[0:norb]
-        rest = value[24:32]
-        out[0:8, 128:160] = rest[:, 0:32]
-        out[8:16, 128:160] = pltpu.roll(rest, 96, 1)[:, 0:32]
-        out[16:20, 128:160] = pltpu.roll(rest, 64, 1)[0:4, 0:32]
+        sums_ref[which] = ordered(gy_in.at[which], ngy) * scale
 
     z_done(0).wait_recv()
     scatter(0, product(operand(0), operand(0)))
-    over_gx(0)
     z_done(1).wait_recv()
     one_way = product(operand(0), operand(1))
     scatter(1, one_way + one_way.T)
+    over_gx(0)
     over_gy(0)
     over_gx(1)
-    finish(0, corr_ref)
+    finish(0)
     over_gy(1)
-    finish(1, proj_ref)
+    finish(1)
 
     for level in range(4):
         for side in range(4):
@@ -377,6 +371,18 @@
     save.wait()
 
 
+def deliver(sums_ref, filt_ref, out_ref, corr_ref, proj_ref):
+    out_ref[...] = filt_ref[...]
+    norb = corr_ref.shape[0]
+    for which, out in enumerate((corr_ref, proj_ref)):
+        value = sums_ref[which]
+        out[:, 0:128] = value[0:norb]
+        rest = value[24:32]
+        out[0:8, 128:160] = rest[:, 0:32]
+        out[8:16, 128:160] = pltpu.roll(rest, 96, 1)[:, 0:32]
+        out[16:20, 128:160] = pltpu.roll(rest, 64, 1)[0:4, 0:32]
+
+
 def body(orbitals, potential):
     norb, wx, wy, nz = orbitals.shape
     ngx, ngy, nb = lax.axis_size("gx"), lax.axis_size("gy"), lax.axis_size("band")
@@ -386,15 +392,14 @@
     block = (norb, wx, wy, nz)
     vmem = pl.BlockSpec(memory_space=pltpu.VMEM)
     hbm = pl.BlockSpec(memory_space=pltpu.HBM)
-    return pl.pallas_call(
+    filtered, sums = pl.pallas_call(
         functools.partial(kernel, (ngx, ngy, nb), scale),
         out_shape=(
             jax.ShapeDtypeStruct(block, F32),
-            jax.ShapeDtypeStruct((norb, total), F32),
-            jax.ShapeDtypeStruct((norb, total), F32),
+            jax.ShapeDtypeStruct((2, 32, 128), F32),
         ),
         in_specs=[hbm, hbm],
-        out_specs=(hbm, vmem, vmem),
+        out_specs=(hbm, vmem),
         scratch_shapes=[
             pltpu.VMEM((5,) + block, F32),
             pltpu.VMEM((4, norb, wx, 24, nz), F32),
@@ -421,10 +426,21 @@
             pltpu.SemaphoreType.DMA((2, 2)),
         ],
         compiler_params=pltpu.CompilerParams(
-            collective_id=0, has_side_effects=True, vmem_limit_bytes=48 * 1024 * 1024
+            collective_id=0, has_side_effects=True, vmem_limit_bytes=60 * 1024 * 1024
         ),
         cost_estimate=pl.CostEstimate(flops=200_000_000, bytes_accessed=2_000_000, transcendentals=0),
     )(orbitals, potential)
+    return pl.pallas_call(
+        deliver,
+        out_shape=(
+            jax.ShapeDtypeStruct(block, F32),
+            jax.ShapeDtypeStruct((norb, total), F32),
+            jax.ShapeDtypeStruct((norb, total), F32),
+        ),
+        in_specs=[vmem, vmem],
+        out_specs=(vmem, vmem, vmem),
+        cost_estimate=pl.CostEstimate(flops=10_000, bytes_accessed=1_000_000, transcendentals=0),
+    )(sums, filtered)
 
 
 def solution(mesh):

time: 75.6 us -> 68.2 us (0.902)
  local copies, waits for them, and re-layouts: 3.76 us -> 0 us
  Pallas kernels: 71 us -> 67.5 us
    pallas_call x1, Pallas kernels: 71 us -> 65.6 us  [body(): pl.pallas_call(functools.partial(kernel, (ngx, ngy, nb), scale), out_shap...]
    unnamed x7 -> x0, local copies, waits for them, and re-layouts: 3.76 us -> none
    pallas_call x0 -> x1, Pallas kernels: none -> 1.87 us  [body(): pl.pallas_call(deliver, out_shape=(jax.ShapeDtypeStruct(block, F32), jax....]
where the time goes in v2:
time: 68.2 us; the launch traced here: 68.1 us
  Pallas kernels  67.5 us (99%)
    pallas_call x1, Pallas kernels, body(): pl.pallas_call(functools.partial(kernel, (ngx, ngy, nb), scale), out_shap...  65.6 us
    pallas_call x1, Pallas kernels, body(): pl.pallas_call(deliver, out_shape=(jax.ShapeDtypeStruct(block, F32), jax....  1.87 us

profile of v2, /device:TPU:1, one launch (start us, length us, event | category | flops | bytes accessed | tf_op | source)
XLA Modules:
  0.0 68.1 jit_solution(13088150772175147024)
XLA Ops:
  0.6 65.6 %shard_map.49 = (f32[20,6,8,128]{3,2,1,0:T(8,128)}, f32[2,32,128]{2,1,0:T(8,128)}) custom-call(f32[20,6,8,128]{3,2,1,0:T(8,128)} %v_ref.1, f32[6,8,128]{2,1,0:T(8,128)} %pot_ref.1), custom_call_target="tpu_custom_call" | custom-call | flops 200000000 | bytes 2000000 | tf_op jit(solution)/shard_map/pallas_call | solution.py:395
  66.2 1.9 %shard_map.50 = (f32[20,6,8,128]{3,2,1,0:T(8,128)}, f32[20,160]{1,0:T(8,128)}, f32[20,160]{1,0:T(8,128)}) custom-call(f32[2,32,128]{2,1,0:T(8,128)} %get-tuple-element.5.sums_ref, f32[20,6,8,128]{3,2,1,0:T(8,128)} %get-tuple-element.6.filt_ref), custom_call_target="tpu_custom_call" | custom-call | flops 10000 | bytes 1000000 | tf_op jit(solution)/shard_map/pallas_call | solution.py:433

commit v3 on v2

--- a/solution.py
+++ b/solution.py
@@ -76,6 +76,10 @@
         {"band": lax.rem(band + nb - 1, nb)},
     )
 
+    barrier = pltpu.get_barrier_semaphore()
+    for peer in sides:
+        pl.semaphore_signal(barrier, 1, device_id=peer, device_id_type=MESH)
+
     def clear(n, carry):
         for x in range(wx):
             xlo[3, n, x, 0:half_y] = jnp.zeros((half_y, nz), F32)
@@ -87,10 +91,6 @@
         return carry
 
     lax.fori_loop(0, norb, clear, 0)
-
-    barrier = pltpu.get_barrier_semaphore()
-    for peer in sides:
-        pl.semaphore_signal(barrier, 1, device_id=peer, device_id_type=MESH)
 
     taps = [0.0] + [-0.5 * w / half_width for w in stencil_weights[1:]]
     lane = lax.broadcasted_iota(jnp.int32, (wy, nz), 1)
@@ -109,23 +109,14 @@
 
     tail[...] = jnp.zeros_like(tail)
     load.wait()
-    load_pot.wait()
-    diag[...] = (diag[...] - 1.5 * stencil_weights[0] - center_level) * (1.0 / half_width)
-
-    def fill(n, carry):
-        for x in range(wx):
-            tall[0, n, x, 8:16] = own[0, n, x]
-        return carry
-
-    lax.fori_loop(0, norb, fill, 0)
     pl.semaphore_wait(barrier, 6)
 
     def relay(turn):
-        for peer in sides:
+        for peer in sides[4:]:
             pl.semaphore_signal(ready.at[turn], 1, device_id=peer, device_id_type=MESH)
 
     def heard(turn):
-        pl.semaphore_wait(ready.at[turn], 6)
+        pl.semaphore_wait(ready.at[turn], 2)
 
     def halo_copy(level, start, count, sem_at, side):
         group = pl.ds(start, count)
@@ -203,7 +194,7 @@
     def spread(which, c, value):
         stage[which, c] = jnp.swapaxes(value, 0, 1)
         gather[which, z_rows(c)] = stage[which, c, band]
-        for d in (1, 2, 3, 4, -1, -2, -3):
+        for d in (4, 3, -3, 2, -2, 1, -1):
             peer = lax.rem(band + d + nb, nb)
             pltpu.make_async_remote_copy(
                 src_ref=stage.at[which, c, peer],
@@ -248,6 +239,15 @@
     cut = (chunks + 1) // 2
     run(-1, 0, cut)
     relay(0)
+    load_pot.wait()
+    diag[...] = (diag[...] - 1.5 * stencil_weights[0] - center_level) * (1.0 / half_width)
+
+    def fill(n, carry):
+        for x in range(wx):
+            tall[0, n, x, 8:16] = own[0, n, x]
+        return carry
+
+    lax.fori_loop(0, norb, fill, 0)
     heard(0)
     relay(1)
     run(0, 0, cut)
@@ -301,7 +301,7 @@
             packed = tail[b, 0:8] + pltpu.roll(tail[b, 8:16], 32, 1) + pltpu.roll(tail[b, 16:24], 64, 1)
             rows_out[which, b, 24:32] = packed
         rows_in[which, band] = rows_out[which, band]
-        for d in (1, 2, 3, 4, -1, -2, -3):
+        for d in (4, 3, -3, 2, -2, 1, -1):
             peer = lax.rem(band + d + nb, nb)
             pltpu.make_async_remote_copy(
                 src_ref=rows_out.at[which, peer],
@@ -321,7 +321,7 @@
     def over_gx(which):
         rows_done(which).wait_recv()
         gx_in[which, gx] = ordered(rows_in.at[which], nb)
-        for d in range(1, ngx):
+        for d in (4, 3, 5, 2, 6, 1, 7):
             pltpu.make_async_remote_copy(
                 src_ref=gx_in.at[which, gx],
                 dst_ref=gx_in.at[which, gx],
@@ -334,7 +334,7 @@
     def over_gy(which):
         gx_done(which).wait_recv()
         gy_in[which, gy] = ordered(gx_in.at[which], ngx)
-        for d in range(1, ngy):
+        for d in (2, 1, 3):
             pltpu.make_async_remote_copy(
                 src_ref=gy_in.at[which, gy],
                 dst_ref=gy_in.at[which, gy],

time: 68.2 us -> 66.8 us (0.979)
  Pallas kernels: 67.5 us -> 66.1 us
    pallas_call x1, Pallas kernels: 65.6 us -> 64.2 us  [body(): pl.pallas_call(functools.partial(kernel, (ngx, ngy, nb), scale), out_shap...]
where the time goes in v3:
time: 66.8 us; the launch traced here: 66.7 us
  Pallas kernels  66.1 us (99%)
    pallas_call x1, Pallas kernels, body(): pl.pallas_call(functools.partial(kernel, (ngx, ngy, nb), scale), out_shap...  64.2 us
    pallas_call x1, Pallas kernels, body(): pl.pallas_call(deliver, out_shape=(jax.ShapeDtypeStruct(block, F32), jax....  1.87 us

profile of v3, /device:TPU:1, one launch (start us, length us, event | category | flops | bytes accessed | tf_op | source)
XLA Modules:
  0.0 66.7 jit_solution(520305488150979408)
XLA Ops:
  0.6 64.2 %shard_map.49 = (f32[20,6,8,128]{3,2,1,0:T(8,128)}, f32[2,32,128]{2,1,0:T(8,128)}) custom-call(f32[20,6,8,128]{3,2,1,0:T(8,128)} %v_ref.1, f32[6,8,128]{2,1,0:T(8,128)} %pot_ref.1), custom_call_target="tpu_custom_call" | custom-call | flops 200000000 | bytes 2000000 | tf_op jit(solution)/shard_map/pallas_call | solution.py:395
  64.8 1.9 %shard_map.50 = (f32[20,6,8,128]{3,2,1,0:T(8,128)}, f32[20,160]{1,0:T(8,128)}, f32[20,160]{1,0:T(8,128)}) custom-call(f32[2,32,128]{2,1,0:T(8,128)} %get-tuple-element.5.sums_ref, f32[20,6,8,128]{3,2,1,0:T(8,128)} %get-tuple-element.6.filt_ref), custom_call_target="tpu_custom_call" | custom-call | flops 10000 | bytes 1000000 | tf_op jit(solution)/shard_map/pallas_call | solution.py:433

commit v4 on v3

--- a/solution.py
+++ b/solution.py
@@ -256,10 +256,12 @@
     run(1, 0, cut)
     run(-1, cut, chunks)
     heard(2)
-    run(2, 0, cut)
+    run(2, 0, cut - 1)
     run(0, cut, chunks)
-    run(3, 0, cut)
+    run(2, cut - 1, cut)
+    run(3, 0, cut - 1)
     run(1, cut, chunks)
+    run(3, cut - 1, cut)
     run(2, cut, chunks)
     save = pltpu.make_async_copy(own.at[3], filt_ref, load_sem.at[0])
     save.start()

time: 66.8 us -> 66.5 us (level)
  no operation moved by 1% of the time
where the time goes in v4:
time: 66.5 us; the launch traced here: 66.4 us
  Pallas kernels  65.7 us (99%)
    pallas_call x1, Pallas kernels, body(): pl.pallas_call(functools.partial(kernel, (ngx, ngy, nb), scale), out_shap...  63.9 us
    pallas_call x1, Pallas kernels, body(): pl.pallas_call(deliver, out_shape=(jax.ShapeDtypeStruct(block, F32), jax....  1.87 us

profile of v4, /device:TPU:1, one launch (start us, length us, event | category | flops | bytes accessed | tf_op | source)
XLA Modules:
  0.0 66.4 jit_solution(13020542354209056398)
XLA Ops:
  0.6 63.9 %shard_map.49 = (f32[20,6,8,128]{3,2,1,0:T(8,128)}, f32[2,32,128]{2,1,0:T(8,128)}) custom-call(f32[20,6,8,128]{3,2,1,0:T(8,128)} %v_ref.1, f32[6,8,128]{2,1,0:T(8,128)} %pot_ref.1), custom_call_target="tpu_custom_call" | custom-call | flops 200000000 | bytes 2000000 | tf_op jit(solution)/shard_map/pallas_call | solution.py:397
  64.5 1.9 %shard_map.50 = (f32[20,6,8,128]{3,2,1,0:T(8,128)}, f32[20,160]{1,0:T(8,128)}, f32[20,160]{1,0:T(8,128)}) custom-call(f32[2,32,128]{2,1,0:T(8,128)} %get-tuple-element.5.sums_ref, f32[20,6,8,128]{3,2,1,0:T(8,128)} %get-tuple-element.6.filt_ref), custom_call_target="tpu_custom_call" | custom-call | flops 10000 | bytes 1000000 | tf_op jit(solution)/shard_map/pallas_call | solution.py:435

commit v5 on v4

--- a/solution.py
+++ b/solution.py
@@ -155,8 +155,8 @@
             device_id_type=MESH,
         )
 
-    def halo_start(level, c):
-        for side in (2, 3, 0, 1):
+    def halo_start(level, c, which=(2, 3, 0, 1)):
+        for side in which:
             halo_copy(level, c * PART, PART, c, side).start()
 
     def halo_wait(level, c):
@@ -226,10 +226,10 @@
         if level >= 2:
             spread(level - 2, c, own[level + 1, pl.ds(c * PART, PART)].reshape(PART * wx, wy, nz))
 
-    def run(level, first, end):
+    def run(level, first, end, which=(2, 3, 0, 1)):
         def body(c, carry):
             if level < 0:
-                halo_start(0, c)
+                halo_start(0, c, which)
             else:
                 step(level, c)
             return carry
@@ -254,7 +254,8 @@
     heard(1)
     relay(2)
     run(1, 0, cut)
-    run(-1, cut, chunks)
+    run(-1, cut, chunks, (2, 3))
+    run(-1, cut, chunks, (0, 1))
     heard(2)
     run(2, 0, cut - 1)
     run(0, cut, chunks)

time: 66.5 us -> 66.5 us (level)
  no operation moved by 1% of the time
where the time goes in v5:
time: 66.5 us; the launch traced here: 66.4 us
  Pallas kernels  65.7 us (99%)
    pallas_call x1, Pallas kernels, body(): pl.pallas_call(functools.partial(kernel, (ngx, ngy, nb), scale), out_shap...  63.9 us
    pallas_call x1, Pallas kernels, body(): pl.pallas_call(deliver, out_shape=(jax.ShapeDtypeStruct(block, F32), jax....  1.87 us

profile of v5, /device:TPU:1, one launch (start us, length us, event | category | flops | bytes accessed | tf_op | source)
XLA Modules:
  0.0 66.4 jit_solution(14562709766056518567)
XLA Ops:
  0.6 63.9 %shard_map.49 = (f32[20,6,8,128]{3,2,1,0:T(8,128)}, f32[2,32,128]{2,1,0:T(8,128)}) custom-call(f32[20,6,8,128]{3,2,1,0:T(8,128)} %v_ref.1, f32[6,8,128]{2,1,0:T(8,128)} %pot_ref.1), custom_call_target="tpu_custom_call" | custom-call | flops 200000000 | bytes 2000000 | tf_op jit(solution)/shard_map/pallas_call | solution.py:398
  64.5 1.9 %shard_map.50 = (f32[20,6,8,128]{3,2,1,0:T(8,128)}, f32[20,160]{1,0:T(8,128)}, f32[20,160]{1,0:T(8,128)}) custom-call(f32[2,32,128]{2,1,0:T(8,128)} %get-tuple-element.5.sums_ref, f32[20,6,8,128]{3,2,1,0:T(8,128)} %get-tuple-element.6.filt_ref), custom_call_target="tpu_custom_call" | custom-call | flops 10000 | bytes 1000000 | tf_op jit(solution)/shard_map/pallas_call | solution.py:436
